TPU v7x, 32 devices: a whole 2x2x4 slice. The times are simulated.
32 devices in a mesh: doc: 2 (over y), seq: 8 (over z, core), head: 2 (over x), sub: 1.
Axes of the slice: x: 2, y: 2, z: 4, core: 2. Of those that a mesh axis runs over, the one named last changes fastest.
Arguments:
- tokens: bfloat16 [8192, 4096], P(('doc', 'seq')), parts along dimension 0, may hold values from -6 to 6
- pre_gain: float32 [4096], replicated, may hold values from 0.5 to 1.5
- w_qkv: bfloat16 [3, 4096, 4096], P(None, 'seq', ('head', 'sub')), may hold values from -0.09375 to 0.09375
- level_index: int32 [128, 32, 7], P(('doc', 'seq'), ('head', 'sub')), parts along dimension 0, may hold values from 0 to 7
- head_gain: float32 [4096], P(('head', 'sub')), may hold values from 0.5 to 1.5
- w_out: bfloat16 [4096, 4096], P(('head', 'sub'), 'seq'), may hold values from -0.125 to 0.125
Outputs:
- layer_out: bfloat16 [8192, 4096], P(('doc', 'seq'), ('head', 'sub')), parts along dimension 0
There are 2 independent parts, one for each index of `doc`. A program takes and returns all parts, laid end to end along the dimension named above; an argument that names none is the same for every part. Nothing has to cross between parts.
Inputs may be any that keep to these rules, and one draw needn't show every extreme that they name: `level_index`: indices into the table of eight level weights.
All inputs are finite; a program needn't handle non-finite values.
Results may differ from a plain program's by a relative error of at most 0.015.
Values may be sent and summed in bfloat16 or wider, within the bound.
A program may use at most 128 MiB of HBM per device.

v0:
```python
import jax
import jax.numpy as jnp
from jax import lax
from jax.sharding import PartitionSpec as P

HD = 128
GROUP = 64


TABLE = (0.25, 0.4, 0.6, 0.8, 1.0, 1.3, 1.7, 2.2)


def partner_2(value, axis, apart):
    mask = 2**apart
    pairs = [(source, source ^ mask) for source in range(lax.axis_size(axis))]
    return lax.ppermute(value, axis, pairs)


def bit_length(numbers):
    counted = jnp.zeros_like(numbers)
    for bit_shift in range(16):
        counted = counted + (numbers >> bit_shift > 0).astype(jnp.int32)
    return counted


def body(tokens, pre_gain, w_qkv, level_index, head_gain, w_out):
    tok_rows = tokens.shape[0]
    widened = tokens.astype(jnp.float32)
    normed = (
        widened * lax.rsqrt(jnp.mean(widened * widened, axis=1, keepdims=True) + 1e-05) * pre_gain
    ).astype(jnp.bfloat16)
    head_cols = w_qkv.shape[2]
    heads_here = head_cols // HD
    groups_here = tok_rows // GROUP
    projected = jnp.einsum(
        "td,kdc->ktc",
        normed,
        lax.all_gather(w_qkv, "seq", axis=1, tiled=True),
        preferred_element_type=jnp.float32,
    ).astype(jnp.bfloat16)
    queries = projected[0].reshape(groups_here, GROUP, heads_here, HD)
    key_rows = projected[1].reshape(groups_here, GROUP, heads_here, HD)
    values = projected[2].reshape(groups_here, GROUP, heads_here, HD)
    level_weight = jnp.zeros(level_index.shape, jnp.float32)
    for entry in range(len(TABLE)):
        level_weight = level_weight + jnp.where(level_index == entry, TABLE[entry], 0.0)
    states = jnp.einsum("cthi,cthj->hcij", key_rows, values, preferred_element_type=jnp.float32)
    local_bits = groups_here.bit_length() - 1
    group_ids = jnp.arange(groups_here, dtype=jnp.int32)
    later_group = group_ids[:, None]
    earlier_group = group_ids[None, :]
    level_of = bit_length(jnp.bitwise_xor(later_group, earlier_group))
    level_ids = jnp.arange(local_bits + 1, dtype=jnp.int32)
    onehot = (
        (level_of[:, :, None] == level_ids[None, None, :])
        & (earlier_group < later_group)[:, :, None]
    ).astype(jnp.float32)
    coefficient = jnp.einsum(
        "ihl,ijl->hij",
        level_weight[:, :, : local_bits + 1],
        onehot,
        precision=lax.Precision.HIGHEST,
    )
    carried = jnp.einsum("hij,hjab->hiab", coefficient, states, precision=lax.Precision.HIGHEST)
    totals = jnp.sum(states, axis=1)
    seq_bits = lax.axis_size("seq").bit_length() - 1
    position = lax.axis_index("seq")
    level_states = []
    block_sum = totals
    for bit_index in range(seq_bits):
        partner = partner_2(block_sum.astype(jnp.bfloat16), "seq", bit_index).astype(
            block_sum.dtype
        )
        upper_half = (position >> bit_index & 1).astype(jnp.float32)
        level_states.append(upper_half * partner)
        block_sum = block_sum + partner
    stacked = jnp.stack(level_states, axis=0)
    carried = carried + jnp.einsum(
        "ihn,nhab->hiab",
        level_weight[:, :, local_bits + 1 :],
        stacked,
        precision=lax.Precision.HIGHEST,
    )
    scaling = HD ** (-0.5)
    positions = jnp.arange(GROUP, dtype=jnp.int32)
    causal = positions[:, None] >= positions[None, :]
    scores = jnp.einsum("cthi,cuhi->hctu", queries, key_rows, preferred_element_type=jnp.float32)
    own_weight = level_weight[:, :, 0].T[:, :, None, None]
    weights = (scores * scaling * own_weight * causal).astype(jnp.bfloat16)
    local_part = jnp.einsum("hctu,cuhi->cthi", weights, values, preferred_element_type=jnp.float32)
    carried_part = (
        jnp.einsum(
            "cthi,hcij->cthj", queries.astype(jnp.float32), carried, precision=lax.Precision.HIGHEST
        )
        * scaling
    )
    attended = local_part + carried_part
    head_scale = head_gain.reshape(heads_here, HD)
    head_normed = (
        attended
        * lax.rsqrt(jnp.mean(attended * attended, axis=3, keepdims=True) + 1e-05)
        * head_scale
    ).astype(jnp.bfloat16)
    head_normed = head_normed.reshape(tok_rows, head_cols)
    feature_cols = w_out.shape[1] * lax.axis_size("seq") // lax.axis_size(("head", "sub"))
    local_terms = jnp.dot(
        head_normed,
        lax.all_gather(w_out, "seq", axis=1, tiled=True),
        preferred_element_type=jnp.float32,
    )
    summed = lax.psum_scatter(
        local_terms.astype(jnp.bfloat16), ("head", "sub"), scatter_dimension=1, tiled=True
    ).astype(jnp.float32)
    residual = lax.dynamic_slice_in_dim(
        widened, lax.axis_index(("head", "sub")) * feature_cols, feature_cols, 1
    )
    return (residual + summed).astype(jnp.bfloat16)


def solution(mesh):
    placed = (
        P(("doc", "seq"), None),
        P(),
        P(None, "seq", ("head", "sub")),
        P(("doc", "seq"), ("head", "sub"), None),
        P(("head", "sub")),
        P(("head", "sub"), "seq"),
    )
    return jax.shard_map(
        body,
        mesh=mesh,
        in_specs=placed,
        out_specs=P(("doc", "seq"), ("head", "sub")),
        check_vma=False,
    )
```

profile of v0, /device:TPU:0, one launch (start us, length us, event | category | flops | bytes accessed | tf_op | source)
XLA Modules:
  0.0 724.2 jit_solution(7479421136152842410)
XLA Ops:
  6.5 0.0 all-gather.3.cloned.1.call-start
  6.5 0.7 all-gather.3.cloned.1.call-update
  7.3 0.0 copy-start.6
  7.3 0.0 all-gather.5.cloned.1.call-start
  7.3 0.7 all-gather.5.cloned.1.call-update
  8.0 0.0 reduce-scatter.2.cloned.1.call-start
  8.1 3.1 multiply_reduce_fusion
  11.2 427.9 %all-gather.3.cloned.1.call-done = bf16[3,4096,2048]{2,1,0:T(8,128)(2,1)} async-done(((bf16[3,512,2048]{2,1,0:T(8,128)(2,1)}), bf16[3,4096,2048]{2,1,0:T(8,128)(2,1)}) %all-gather.3.cloned.1.call-update) | async-done | bytes 50331664 | tf_op jit(solution)/shard_map/all_gather | solution.py:38
  439.1 0.0 copy-done.6
  439.1 32.6 %convert_bitcast_fusion = bf16[3,512,2048]{2,1,0:T(8,128)(2,1)S(1)} fusion(bf16[3,4096,2048]{2,1,0:T(8,128)(2,1)} %all-gather.3.cloned.1.call-done, f32[4096]{0:T(1024)S(1)} %copy-done.6, f32[512]{0:T(512)S(1)} %add_rsqrt_fusion.1, bf16[512,4096]{1,0:T(8,128)(2,1)} %param.6), kind=kOutput, calls=%fused_computation.7 | convolution fusion | flops 25781338112 | bytes 60835840 | tf_op jit(solution)/shard_map/td,kdc->ktc/dot_general | solution.py:35
  471.7 4.0 slice_bitcast_fusion.2
  475.7 0.6 copy.25
  476.3 0.0 copy-start.1
  476.3 0.6 copy.26
  476.9 0.0 copy-start.2
  477.0 0.0 copy-start.4
  477.0 5.6 fusion.38
  482.6 0.0 copy-done.1
  482.6 0.0 copy-done.2
  482.6 0.1 convert_element_type.198
  482.6 0.3 collective-permute-start
  483.0 0.0 copy-done.4
  483.0 0.1 copy.21
  483.1 1.5 collective-permute-done
  484.6 0.0 copy-start.3
  484.6 1.0 fusion.30
  485.6 0.0 collective-permute-start.1
  485.7 0.2 convolution_bitcast_fusion
  485.9 0.1 copy.18
  486.0 0.0 copy-done.3
  486.0 0.0 copy-start
  486.0 2.3 copy.24
  488.4 56.9 %collective-permute-done.1 = bf16[16,128,128]{2,1,0:T(8,128)(2,1)} collective-permute-done((bf16[16,128,128]{2,1,0:T(8,128)(2,1)}, bf16[16,128,128]{2,1,0:T(8,128)(2,1)}, u32[]{:S(2)}, u32[]{:S(2)}) %collective-permute-start.1) | collective-permute-done | bytes 524320 | tf_op jit(solution)/shard_map/ppermute | solution.py:16
  545.3 1.5 fusion.27
  546.8 0.1 collective-permute-start.2
  546.9 0.0 copy-done
  546.9 12.7 %fusion.2 = f32[16,8,128,128]{3,1,2,0:T(8,128)} fusion(f32[16,8,8,1]{2,1,3,0:T(8,128)S(1)} %copy.18, f32[16,8,128,128]{3,2,1,0:T(8,128)S(1)} %copy-done), kind=kOutput, calls=%fused_computation.3 | convolution fusion | flops 201326592 | bytes 16781312 | tf_op jit(solution)/shard_map/hij,hjab->hiab/dot_general | solution.py:64
  559.7 46.7 %collective-permute-done.2 = bf16[16,128,128]{2,1,0:T(8,128)(2,1)S(1)} collective-permute-done((bf16[16,128,128]{2,1,0:T(8,128)(2,1)S(1)}, bf16[16,128,128]{2,1,0:T(8,128)(2,1)S(1)}, u32[]{:S(2)}, u32[]{:S(2)}) %collective-permute-start.2) | collective-permute-done | bytes 524320 | tf_op jit(solution)/shard_map/ppermute | solution.py:16
  606.4 0.1 multiply_bitcast_fusion
  606.5 0.3 pad_maximum_fusion
  606.7 12.1 %fusion.9 = f32[16,8,128,128]{3,1,2,0:T(8,128)} fusion(f32[8,16,3,1]{0,2,3,1:T(4,128)S(1)} %copy.21, f32[3,16,128,128]{3,2,1,0:T(8,128)S(1)} %pad_maximum_fusion), kind=kOutput, calls=%fused_computation.15 | convolution fusion | flops 75497472 | bytes 11535872 | tf_op jit(solution)/shard_map/ihn,nhab->hiab/dot_general | solution.py:78
  618.9 14.2 %fusion = f32[8,16,128,64]{2,3,1,0:T(8,128)} fusion(f32[16,8,128,128]{3,1,2,0:T(8,128)} %fusion.9, f32[16,8,128,128]{3,1,2,0:T(8,128)} %fusion.2, bf16[8,64,16,128]{3,2,1,0:T(8,128)(2,1)S(1)} %bitcast.55), kind=kOutput, calls=%fused_computation.1 | convolution fusion | flops 1612709888 | bytes 23068672 | tf_op jit(solution)/shard_map/cthi,hcij->cthj/dot_general | solution.py:92
  633.1 0.0 copy-start.5
  633.1 7.8 %fusion.6 = (f32[8,64,16]{1,2,0:T(8,128)S(1)}, f32[8,16,128,64]{2,3,1,0:T(8,128)}) fusion(f32[8,16,128,64]{2,3,1,0:T(8,128)} %fusion, bf16[8,64,16,128]{3,2,1,0:T(8,128)(2,1)} %bitcast.60, bf16[8,64,16,128]{3,2,1,0:T(8,128)(2,1)} %bitcast.58, f32[64,64]{1,0:T(8,128)S(1)} %fusion.31, f32[16,8]{0,1:T(8,128)S(1)} %fusion.37, ...), kind=kOutput, calls=%fused_computation.12 | convolution fusion | flops 274194432 | bytes 14729728 | tf_op jit(solution)/shard_map/hctu,cuhi->cthi/dot_general | solution.py:90
  640.8 0.0 copy-done.5
  640.9 2.9 fusion.8
  643.8 1.4 copy.15
  645.1 0.0 all-gather.5.cloned.1.call-done
  645.2 14.0 %convolution_convert_fusion = bf16[512,4096]{1,0:T(8,128)(2,1)} fusion(bf16[2048,4096]{1,0:T(8,128)(2,1)} %all-gather.5.cloned.1.call-done, bf16[64,8,16,128]{3,2,1,0:T(8,128)(2,1)S(1)} %bitcast.61), kind=kOutput, calls=%fused_computation.8 | convolution fusion | flops 8592031744 | bytes 23068672 | tf_op jit(solution)/shard_map/dot_general | solution.py:106
  659.2 0.0 reduce-scatter.2.cloned.1.call-update
  659.2 6.8 convert_element_type.175
  666.0 46.4 %reduce-scatter.2.cloned.1.call-done = bf16[512,2048]{1,0:T(8,128)(2,1)} async-done(((bf16[512,4096]{1,0:T(8,128)(2,1)}), bf16[512,2048]{1,0:T(8,128)(2,1)}) %reduce-scatter.2.cloned.1.call-update) | async-done | bytes 2097168 | tf_op jit(solution)/shard_map/reduce_scatter | solution.py:111
  712.4 4.8 add_convert_fusion
  (9 shorter events, 0.1 us)
Async XLA Ops:
  6.5 432.6 %all-gather.3.cloned.1.call-start = ((), (), s32[]{:S(2)}) async-start(), calls=%async_computation.1 | async-start | bytes 56623104 | tf_op jit(solution)/shard_map/all_gather | solution.py:38
  7.3 431.9 %copy-start.6 = (f32[4096]{0:T(1024)S(1)}, f32[4096]{0:T(1024)}, u32[]{:S(2)}) copy-start(f32[4096]{0:T(1024)} %param.7) | copy-start | bytes 49156
  7.3 637.9 %all-gather.5.cloned.1.call-start = ((), (), s32[]{:S(2)}) async-start(), calls=%async_computation.2 | async-start | bytes 18874368 | tf_op jit(solution)/shard_map/all_gather | solution.py:108
  8.0 704.4 %reduce-scatter.2.cloned.1.call-start = ((), (), s32[]{:S(2)}) async-start(), calls=%async_computation.3 | async-start | bytes 6291456 | tf_op jit(solution)/shard_map/reduce_scatter | solution.py:111
  476.3 6.2 copy-start.1
  476.9 5.6 copy-start.2
  477.0 6.0 copy-start.4
  482.6 2.0 collective-permute-start
  484.6 1.4 copy-start.3
  485.6 59.7 %collective-permute-start.1 = (bf16[16,128,128]{2,1,0:T(8,128)(2,1)}, bf16[16,128,128]{2,1,0:T(8,128)(2,1)}, u32[]{:S(2)}, u32[]{:S(2)}) collective-permute-start(bf16[16,128,128]{2,1,0:T(8,128)(2,1)} %fusion.30), channel_id=1, source_target_pairs={{0,4},{2,6},{4,0},{6,2},{8,12},{10,14},{12,8},{14,10},{1,5},{3,7},... | collective-permute-start | bytes 1572872 | tf_op jit(solution)/shard_map/ppermute | solution.py:16
  486.0 60.9 %copy-start = (f32[16,8,128,128]{3,2,1,0:T(8,128)S(1)}, f32[16,8,128,128]{3,2,1,0:T(8,128)}, u32[]{:S(2)}) copy-start(f32[16,8,128,128]{3,2,1,0:T(8,128)} %get-tuple-element.12) | copy-start | bytes 25165828
  546.8 59.5 %collective-permute-start.2 = (bf16[16,128,128]{2,1,0:T(8,128)(2,1)S(1)}, bf16[16,128,128]{2,1,0:T(8,128)(2,1)S(1)}, u32[]{:S(2)}, u32[]{:S(2)}) collective-permute-start(bf16[16,128,128]{2,1,0:T(8,128)(2,1)S(1)} %get-tuple-element.9), channel_id=1, source_target_pairs={{0,8},{2,10},{4,12},{6,14},{8,0},{10,2},{12,4},{14,6},{1,9},{3,11}... | collective-permute-start | bytes 1572872 | tf_op jit(solution)/shard_map/ppermute | solution.py:16
  633.1 7.8 %copy-start.5 = (f32[2048]{0:T(1024)S(1)}, f32[2048]{0:T(1024)}, u32[]{:S(2)}) copy-start(f32[2048]{0:T(1024)} %param.10) | copy-start | bytes 24580
Sparse Core Ops, SparseCore 0:
  9.0 430.0 all-gather.2
  440.7 171.6 all-gather.4
  659.3 53.0 reduce-scatter.1
where the time goes:
time: 732 us; the launch traced here: 724 us
  waiting for transfers between devices  581 us (79%)
  matrix products  99.2 us (14%)
  other arithmetic  20.7 us (3%)
  between operations  13.8 us (2%)
  local copies, waits for them, and re-layouts  9.11 us (1%)
    all_gather x1, waiting for transfers between devices, body(): lax.all_gather(w_qkv, 'seq', axis=1, tiled=True)  428 us
    ppermute x3, waiting for transfers between devices, partner_2(): return lax.ppermute(value, axis, pairs)  105 us
    reduce_scatter x1, waiting for transfers between devices, body(): lax.psum_scatter(local_terms.astype(jnp.bfloat16), ('head', 'sub'), scatt...  46.4 us
    dot_general x1, matrix products, body(): jnp.einsum('td,kdc->ktc', normed, lax.all_gather(w_qkv, 'seq', axis=1, ti...  32.6 us
  transfers between devices with their start and end apart: 6, of which 5 were waited for; matrix products, arithmetic and copies ran while one was open for 15% of the time, Pallas kernels for 0%

commit v1 on v0

v1 whole, which is shorter than its diff:
```python
import functools

import jax
import jax.numpy as jnp
from jax import lax
from jax.experimental import pallas as pl
from jax.experimental.pallas import tpu as pltpu
from jax.sharding import PartitionSpec as P

HD = 128
GROUP = 64


TABLE = (0.25, 0.4, 0.6, 0.8, 1.0, 1.3, 1.7, 2.2)


def partner_2(value, axis, apart):
    mask = 2**apart
    pairs = [(source, source ^ mask) for source in range(lax.axis_size(axis))]
    return lax.ppermute(value, axis, pairs)


def bit_length(numbers):
    counted = jnp.zeros_like(numbers)
    for bit_shift in range(16):
        counted = counted + (numbers >> bit_shift > 0).astype(jnp.int32)
    return counted


def head_rows(local_bits, query, keys, values, row_weight, partners, gain):
    rows = query.shape[0]
    scores = lax.dot_general(
        query, keys, (((1,), (1,)), ((), ())), preferred_element_type=jnp.float32
    )
    later = lax.broadcasted_iota(jnp.int32, (rows, rows), 0)
    earlier = lax.broadcasted_iota(jnp.int32, (rows, rows), 1)
    apart = later ^ earlier
    factor = row_weight[:, local_bits : local_bits + 1]
    for level in range(local_bits - 1, -1, -1):
        factor = jnp.where(apart < GROUP << level, row_weight[:, level : level + 1], factor)
    weights = jnp.where(later >= earlier, scores * factor, 0.0).astype(jnp.bfloat16)
    attended = jnp.dot(weights, values, preferred_element_type=jnp.float32)
    for bit_index, partner in enumerate(partners):
        level = local_bits + 1 + bit_index
        attended += row_weight[:, level : level + 1] * jnp.dot(
            query, partner, preferred_element_type=jnp.float32
        )
    mean_square = jnp.mean(attended * attended, axis=1, keepdims=True)
    return (attended * lax.rsqrt(mean_square + 1e-05) * gain).astype(jnp.bfloat16)


def head_kernel(local_bits, q_ref, k_ref, v_ref, weight_ref, partner_ref, gain_ref, out_ref):
    out_ref[...] = head_rows(
        local_bits,
        q_ref[...],
        k_ref[...],
        v_ref[...],
        weight_ref[0],
        [partner_ref[n, 0] for n in range(partner_ref.shape[0])],
        gain_ref[...],
    )


def gathered(weight, axis):
    docs = lax.axis_size("doc")
    part = weight.shape[axis] // docs
    mine = lax.dynamic_slice_in_dim(weight, lax.axis_index("doc") * part, part, axis)
    return lax.all_gather(mine, ("doc", "seq"), axis=0)


def body(tokens, pre_gain, w_qkv, level_index, head_gain, w_out):
    tok_rows, width = tokens.shape
    docs, seqs = lax.axis_size("doc"), lax.axis_size("seq")
    widened = tokens.astype(jnp.float32)
    normed = (
        widened * lax.rsqrt(jnp.mean(widened * widened, axis=1, keepdims=True) + 1e-05) * pre_gain
    ).astype(jnp.bfloat16)
    head_cols = w_qkv.shape[2]
    groups_here = tok_rows // GROUP
    swapped = normed.reshape(tok_rows, seqs, docs, -1).swapaxes(1, 2).reshape(tok_rows, width)

    def project(which):
        matrix = gathered(w_qkv[which], 0).reshape(width, head_cols)
        return jnp.dot(swapped, matrix, preferred_element_type=jnp.float32).astype(jnp.bfloat16)

    key_rows, values, queries = project(1), project(2), project(0)
    w_out, _ = lax.optimization_barrier((w_out, values))
    out_matrix = gathered(w_out, 0)
    return attend(
        widened, queries, key_rows, values, level_index, head_gain, out_matrix, groups_here
    )


def attend(widened, queries, key_rows, values, level_index, head_gain, out_matrix, groups_here):
    tok_rows = queries.shape[0]
    heads_here = queries.shape[1] // HD
    level_weight = jnp.zeros(level_index.shape, jnp.float32)
    for entry in range(len(TABLE)):
        level_weight = level_weight + jnp.where(level_index == entry, TABLE[entry], 0.0)
    totals = jnp.einsum(
        "thi,thj->hij",
        key_rows.reshape(tok_rows, heads_here, HD),
        values.reshape(tok_rows, heads_here, HD),
        preferred_element_type=jnp.float32,
    )
    local_bits = groups_here.bit_length() - 1
    seq_bits = lax.axis_size("seq").bit_length() - 1
    position = lax.axis_index("seq")
    partners = []
    block_sum = totals
    for bit_index in range(seq_bits):
        partner = partner_2(block_sum.astype(jnp.bfloat16), "seq", bit_index)
        partners.append(partner)
        block_sum = block_sum + partner.astype(jnp.float32)
    bits = jnp.arange(seq_bits, dtype=jnp.int32)
    used = jnp.concatenate(
        [jnp.ones((local_bits + 1,), jnp.int32), position >> bits & 1]
    ).astype(jnp.float32) * HD ** (-0.5)
    row_weights = jnp.repeat((level_weight * used).swapaxes(0, 1), GROUP, axis=1)
    head_normed = pl.pallas_call(
        functools.partial(head_kernel, local_bits),
        grid=(heads_here,),
        in_specs=[pl.BlockSpec((tok_rows, HD), lambda h: (0, h))] * 3
        + [
            pl.BlockSpec((1,) + row_weights.shape[1:], lambda h: (h, 0, 0)),
            pl.BlockSpec((seq_bits, 1, HD, HD), lambda h: (0, h, 0, 0)),
            pl.BlockSpec((1, HD), lambda h: (0, h)),
        ],
        out_specs=pl.BlockSpec((tok_rows, HD), lambda h: (0, h)),
        out_shape=jax.ShapeDtypeStruct((tok_rows, heads_here * HD), jnp.bfloat16),
        compiler_params=pltpu.CompilerParams(vmem_limit_bytes=32 * 2**20),
        cost_estimate=pl.CostEstimate(
            flops=heads_here * tok_rows * HD * 4 * (tok_rows + HD * seq_bits),
            bytes_accessed=tok_rows * heads_here * HD * 12,
            transcendentals=0,
        ),
    )(queries, key_rows, values, row_weights, jnp.stack(partners), head_gain[None, :])
    docs = lax.axis_size("doc")
    split_rows = head_normed.reshape(tok_rows, docs, heads_here * HD // docs)
    local_terms = jnp.einsum(
        "tyk,yskc->tsc",
        split_rows,
        out_matrix.reshape(docs, -1, *out_matrix.shape[1:]),
        preferred_element_type=jnp.float32,
    ).reshape(tok_rows, -1)
    feature_cols = local_terms.shape[1] // lax.axis_size(("head", "sub"))
    summed = lax.psum_scatter(
        local_terms.astype(jnp.bfloat16), ("head", "sub"), scatter_dimension=1, tiled=True
    ).astype(jnp.float32)
    residual = lax.dynamic_slice_in_dim(
        widened, lax.axis_index(("head", "sub")) * feature_cols, feature_cols, 1
    )
    return (residual + summed).astype(jnp.bfloat16)


def solution(mesh):
    placed = (
        P(("doc", "seq"), None),
        P(),
        P(None, "seq", ("head", "sub")),
        P(("doc", "seq"), ("head", "sub"), None),
        P(("head", "sub")),
        P(("head", "sub"), "seq"),
    )
    return jax.shard_map(
        body,
        mesh=mesh,
        in_specs=placed,
        out_specs=P(("doc", "seq"), ("head", "sub")),
        check_vma=False,
    )
```

time: 732 us -> 656 us (0.90)
  waiting for transfers between devices: 581 us -> 485 us
  local copies, waits for them, and re-layouts: 9.11 us -> 60.2 us
  matrix products: 99.2 us -> 58.7 us
  Pallas kernels: 0 us -> 13.1 us
    ppermute x3, waiting for transfers between devices: 105 us -> 35.6 us  [partner_2(): return lax.ppermute(value, axis, pairs)]
    reshape x0 -> x4, local copies, waits for them, and re-layouts: none -> 43.4 us  [the longest x1 21.8 us: attend(): out_matrix.reshape(docs, -1, *out_matrix.shape[1:])]
    dot_general x8 -> x5, matrix products: 99.2 us -> 58.7 us  [the longest x3 41.9 us: project(): jnp.dot(swapped, matrix, preferred_element_type=jnp.float32)]
    all_gather x2 -> x4, waiting for transfers between devices: 428 us -> 404 us  [gathered(): return lax.all_gather(mine, ('doc', 'seq'), axis=0)]
    pallas_call x0 -> x1, Pallas kernels: none -> 13.1 us  [attend(): pl.pallas_call(functools.partial(head_kernel, local_bits), grid=(heads_he...]
    dynamic_slice x0 -> x4, local copies, waits for them, and re-layouts: none -> 8.03 us  [gathered(): lax.dynamic_slice_in_dim(weight, lax.axis_index('doc') * part, part, axis)]
  transfers between devices with their start and end apart: 6 -> 8, of which waited for: 5 -> 7; matrix products, arithmetic and copies ran while one was open for 15% -> 14% of each run, Pallas kernels for 0% -> 2%
where the time goes in v1:
time: 656 us; the launch traced here: 655 us
  waiting for transfers between devices  485 us (74%)
  local copies, waits for them, and re-layouts  60.2 us (9%)
  matrix products  58.7 us (9%)
  other arithmetic  23.2 us (4%)
  between operations  13.3 us (2%)
  Pallas kernels  13.1 us (2%)
    all_gather x4, waiting for transfers between devices, gathered(): return lax.all_gather(mine, ('doc', 'seq'), axis=0)  404 us
    reduce_scatter x1, waiting for transfers between devices, attend(): lax.psum_scatter(local_terms.astype(jnp.bfloat16), ('head', 'sub'), scatt...  45.9 us
    dot_general x3, matrix products, project(): jnp.dot(swapped, matrix, preferred_element_type=jnp.float32)  41.9 us
    ppermute x3, waiting for transfers between devices, partner_2(): return lax.ppermute(value, axis, pairs)  35.6 us
    reshape x1, local copies, waits for them, and re-layouts, attend(): out_matrix.reshape(docs, -1, *out_matrix.shape[1:])  21.8 us
    reshape x2, local copies, waits for them, and re-layouts, body(): normed.reshape(tok_rows, seqs, docs, -1).swapaxes(1, 2)  19 us
    dot_general x1, matrix products, attend(): jnp.einsum('tyk,yskc->tsc', split_rows, out_matrix.reshape(docs, -1, *out...  13.8 us
  transfers between devices with their start and end apart: 8, of which 7 were waited for; matrix products, arithmetic and copies ran while one was open for 14% of the time, Pallas kernels for 2%

profile of v1, /device:TPU:0, one launch (start us, length us, event | category | flops | bytes accessed | tf_op | source)
XLA Modules:
  0.0 654.8 jit_solution(2098688620522117092)
XLA Ops:
  6.5 0.0 copy-start
  6.5 0.0 all-gather.10.cloned.1.call-start
  6.5 5.9 fusion.6
  12.5 2.3 constant_dynamic-slice_fusion.1
  14.8 0.0 all-gather.10.cloned.1.call-update
  14.8 0.0 all-gather.8.cloned.1.call-start
  14.8 2.3 constant_dynamic-slice_fusion.2
  17.2 0.0 copy-start.10
  17.2 0.0 all-gather.8.cloned.1.call-update
  17.2 0.0 all-gather.6.cloned.1.call-start
  17.3 2.3 constant_dynamic-slice_fusion.3
  19.6 0.0 all-gather.6.cloned.1.call-update
  19.6 0.0 all-gather.12.cloned.1.call-start
  19.7 0.0 copy-start.6
  19.7 3.2 multiply_reduce_fusion
  22.9 0.0 copy-done.10
  22.9 0.2 copy-done.6
  23.1 3.7 multiply_convert_fusion
  26.8 7.9 %reshape.48 = bf16[512,8,2,256]{3,2,1,0:T(2,128)(2,1)} reshape(bf16[512,4096]{1,0:T(8,128)(2,1)} %multiply_convert_fusion) | data formatting | bytes 8388608 | tf_op jit(solution)/shard_map/reshape | solution.py:80
  34.7 11.2 %copy.18 = bf16[512,8,2,256]{0,3,1,2:T(8,128)(2,1)} copy(bf16[512,8,2,256]{3,2,1,0:T(2,128)(2,1)} %reshape.48) | data formatting | bytes 8388608 | tf_op jit(solution)/shard_map/reshape | solution.py:80
  45.9 98.7 %all-gather.10.cloned.1.call-done = bf16[16,256,2048]{2,1,0:T(8,128)(2,1)} async-done(((bf16[1,256,2048]{2,1,0:T(8,128)(2,1)}), bf16[16,256,2048]{2,1,0:T(8,128)(2,1)}) %all-gather.10.cloned.1.call-update) | async-done | bytes 16777232 | tf_op jit(solution)/shard_map/all_gather | solution.py:68
  144.5 14.6 %convolution_convert_fusion.v_ref = bf16[512,2048]{1,0:T(8,128)(2,1)} fusion(bf16[512,4096]{0,1:T(8,128)(2,1)} %bitcast.48, bf16[4096,2048]{1,0:T(8,128)(2,1)} %bitcast.54), kind=kOutput, calls=%fused_computation.4 | convolution fusion | flops 8590983168 | bytes 23068672 | tf_op jit(solution)/shard_map/dot_general | solution.py:84
  159.1 0.0 copy-done
  159.1 1.1 constant_dynamic-slice_fusion
  160.2 0.0 all-gather.12.cloned.1.call-update
  160.2 0.2 reduce-scatter.2.cloned.1.call-start
  160.4 111.4 %all-gather.8.cloned.1.call-done = bf16[16,256,2048]{2,1,0:T(8,128)(2,1)} async-done(((bf16[1,256,2048]{2,1,0:T(8,128)(2,1)}), bf16[16,256,2048]{2,1,0:T(8,128)(2,1)}) %all-gather.8.cloned.1.call-update) | async-done | bytes 16777232 | tf_op jit(solution)/shard_map/all_gather | solution.py:68
  271.8 13.6 %convolution_convert_fusion.1.k_ref = bf16[512,2048]{1,0:T(8,128)(2,1)S(1)} fusion(bf16[512,4096]{0,1:T(8,128)(2,1)} %bitcast.49, bf16[4096,2048]{1,0:T(8,128)(2,1)} %bitcast.53), kind=kOutput, calls=%fused_computation.5 | convolution fusion | flops 8590983168 | bytes 23068672 | tf_op jit(solution)/shard_map/dot_general | solution.py:84
  285.5 2.5 copy.24
  288.0 3.0 fusion.7
  291.0 0.3 collective-permute-start
  291.3 1.6 collective-permute-done
  293.0 0.8 copy-done.7
  293.8 0.9 fusion.5
  294.7 0.0 collective-permute-start.1
  294.7 0.1 convert_multiply_fusion
  294.8 0.0 copy-done.9
  294.8 0.1 multiply_bitcast_fusion
  294.9 0.1 copy.19
  295.0 33.9 %collective-permute-done.1 = bf16[16,128,128]{2,1,0:T(8,128)(2,1)} collective-permute-done((bf16[16,128,128]{2,1,0:T(8,128)(2,1)}, bf16[16,128,128]{2,1,0:T(8,128)(2,1)}, u32[]{:S(2)}, u32[]{:S(2)}) %collective-permute-start.1) | collective-permute-done | bytes 524320 | tf_op jit(solution)/shard_map/ppermute | solution.py:20
  328.9 2.2 add_convert_fusion.1
  331.1 0.5 collective-permute-start.2
  331.6 95.5 %all-gather.6.cloned.1.call-done = bf16[16,256,2048]{2,1,0:T(8,128)(2,1)} async-done(((bf16[1,256,2048]{2,1,0:T(8,128)(2,1)}), bf16[16,256,2048]{2,1,0:T(8,128)(2,1)}) %all-gather.6.cloned.1.call-update) | async-done | bytes 16777232 | tf_op jit(solution)/shard_map/all_gather | solution.py:68
  427.1 13.7 %convolution_convert_fusion.2.q_ref = bf16[512,2048]{1,0:T(8,128)(2,1)S(1)} fusion(bf16[512,4096]{0,1:T(8,128)(2,1)} %bitcast.50, bf16[4096,2048]{1,0:T(8,128)(2,1)} %bitcast.52), kind=kOutput, calls=%fused_computation.6 | convolution fusion | flops 8590983168 | bytes 23068672 | tf_op jit(solution)/shard_map/dot_general | solution.py:84
  440.8 0.0 copy-start.2
  440.8 0.0 copy-start.5
  440.8 0.0 collective-permute-done.2
  440.8 0.0 copy-done.8
  440.8 1.4 pad_maximum_fusion.partner_ref
  442.2 0.3 broadcast_in_dim.54
  442.5 0.1 copy-done.2
  442.5 0.0 copy-done.5
  442.5 13.1 %shard_map.64 = bf16[512,2048]{1,0:T(8,128)(2,1)S(1)} custom-call(bf16[512,2048]{1,0:T(8,128)(2,1)S(1)} %convolution_convert_fusion.2.q_ref, bf16[512,2048]{1,0:T(8,128)(2,1)S(1)} %convolution_convert_fusion.1.k_ref, bf16[512,2048]{1,0:T(8,128)(2,1)S(1)} %copy-done.2, f32[16,512,7]{2,1,0:T(8,128)S(1)} %bitcast.41, ...), custom_call_target="tpu_custom_call" | custom-call | flops 3758096384 | bytes 12582912 | tf_op jit(solution)/shard_map/pallas_call | solution.py:120
  455.6 0.0 copy-start.3
  455.7 1.3 copy-done.3
  457.0 98.1 %all-gather.12.cloned.1.call-done = bf16[16384,512]{1,0:T(8,128)(2,1)} async-done(((bf16[1024,512]{1,0:T(8,128)(2,1)}), bf16[16384,512]{1,0:T(8,128)(2,1)}) %all-gather.12.cloned.1.call-update) | async-done | bytes 16777232 | tf_op jit(solution)/shard_map/all_gather | solution.py:68
  555.1 21.8 %copy.22 = bf16[2,8,1024,512]{2,3,1,0:T(8,128)(2,1)} copy(bf16[2,8,1024,512]{3,2,1,0:T(8,128)(2,1)} %bitcast.44) | data formatting | bytes 33554432 | tf_op jit(solution)/shard_map/reshape | solution.py:143
  577.0 0.0 copy-done.4
  577.0 13.8 %bitcast_convert_fusion = bf16[512,4096]{1,0:T(8,128)(2,1)} fusion(bf16[4096,1024,2]{1,0,2:T(8,128)(2,1)} %bitcast.45, bf16[64,2,8,1024]{3,2,1,0:T(8,128)(2,1)S(1)} %bitcast.42), kind=kOutput, calls=%fused_computation | convolution fusion | flops 8592031744 | bytes 23068672 | tf_op jit(solution)/shard_map/tyk,yskc->tsc/dot_general | solution.py:140
  590.8 0.0 reduce-scatter.2.cloned.1.call-update
  590.8 6.7 %convert_element_type.42 = f32[512,4096]{1,0:T(8,128)} convert(bf16[512,4096]{1,0:T(8,128)(2,1)} %param.6) | non-fusion elementwise | flops 2097152 | bytes 12582912 | tf_op jit(solution)/shard_map/convert_element_type | solution.py:74
  597.5 45.9 %reduce-scatter.2.cloned.1.call-done = bf16[512,2048]{1,0:T(8,128)(2,1)} async-done(((bf16[512,4096]{1,0:T(8,128)(2,1)}), bf16[512,2048]{1,0:T(8,128)(2,1)}) %reduce-scatter.2.cloned.1.call-update) | async-done | bytes 2097168 | tf_op jit(solution)/shard_map/reduce_scatter | solution.py:147
  643.4 4.8 add_convert_fusion
  648.3 0.0 copy-done.1
  (7 shorter events, 0.0 us)
Async XLA Ops:
  6.5 152.6 %copy-start = (bf16[2048,512]{1,0:T(8,128)(2,1)S(1)}, bf16[2048,512]{1,0:T(8,128)(2,1)}, u32[]{:S(2)}) copy-start(bf16[2048,512]{1,0:T(8,128)(2,1)} %param.11) | copy-start | bytes 6291460
  6.5 138.0 %all-gather.10.cloned.1.call-start = ((), (), s32[]{:S(2)}) async-start(), calls=%async_computation.3 | async-start | bytes 17825792 | tf_op jit(solution)/shard_map/all_gather | solution.py:68
  14.8 257.0 %all-gather.8.cloned.1.call-start = ((), (), s32[]{:S(2)}) async-start(), calls=%async_computation.2 | async-start | bytes 17825792 | tf_op jit(solution)/shard_map/all_gather | solution.py:68
  17.2 5.7 copy-start.10
  17.2 409.9 %all-gather.6.cloned.1.call-start = ((), (), s32[]{:S(2)}) async-start(), calls=%async_computation.1 | async-start | bytes 17825792 | tf_op jit(solution)/shard_map/all_gather | solution.py:68
  19.6 535.5 %all-gather.12.cloned.1.call-start = ((), (), s32[]{:S(2)}) async-start(), calls=%async_computation.5 | async-start | bytes 17825792 | tf_op jit(solution)/shard_map/all_gather | solution.py:68
  19.7 3.5 copy-start.6
  160.2 483.2 %reduce-scatter.2.cloned.1.call-start = ((), (), s32[]{:S(2)}) async-start(), calls=%async_computation.4 | async-start | bytes 6291456 | tf_op jit(solution)/shard_map/reduce_scatter | solution.py:147
  288.0 6.8 %copy-start.9 = (s32[8,16,7]{1,0,2:T(8,128)S(1)}, s32[8,16,7]{1,0,2:T(8,128)}, u32[]{:S(2)}) copy-start(s32[8,16,7]{1,0,2:T(8,128)} %param.9) | copy-start | bytes 10756
  291.0 2.0 collective-permute-start
  293.0 0.8 copy-start.7
  294.7 34.2 %collective-permute-start.1 = (bf16[16,128,128]{2,1,0:T(8,128)(2,1)}, bf16[16,128,128]{2,1,0:T(8,128)(2,1)}, u32[]{:S(2)}, u32[]{:S(2)}) collective-permute-start(bf16[16,128,128]{2,1,0:T(8,128)(2,1)} %fusion.5), channel_id=1, source_target_pairs={{0,4},{2,6},{4,0},{6,2},{8,12},{10,14},{12,8},{14,10},{1,5},{3,7},... | collective-permute-start | bytes 1572872 | tf_op jit(solution)/shard_map/ppermute | solution.py:20
  331.1 109.7 %collective-permute-start.2 = (bf16[16,128,128]{2,1,0:T(8,128)(2,1)}, bf16[16,128,128]{2,1,0:T(8,128)(2,1)S(1)}, u32[]{:S(2)}, u32[]{:S(2)}) collective-permute-start(bf16[16,128,128]{2,1,0:T(8,128)(2,1)} %add_convert_fusion.1), channel_id=1, source_target_pairs={{0,8},{2,10},{4,12},{6,14},{8,0},{10,2},{12,4},{14,6},{1,9},{3,11}... | collective-permute-start | bytes 1572872 | tf_op jit(solution)/shard_map/ppermute | solution.py:20
  427.1 13.7 %copy-start.8 = (bf16[16,128,128]{2,1,0:T(8,128)(2,1)S(1)}, bf16[16,128,128]{2,1,0:T(8,128)(2,1)}, u32[]{:S(2)}) copy-start(bf16[16,128,128]{2,1,0:T(8,128)(2,1)} %copy-done.7) | copy-start | bytes 1572868
  440.8 1.8 copy-start.2
  440.8 1.7 copy-start.5
  455.6 1.3 copy-start.3
  555.1 21.9 %copy-start.4 = (bf16[512,2048]{1,0:T(8,128)(2,1)S(1)}, bf16[512,2048]{1,0:T(8,128)(2,1)}, u32[]{:S(2)}) copy-start(bf16[512,2048]{1,0:T(8,128)(2,1)} %copy-done.3) | copy-start | bytes 6291460
  597.5 50.8 %copy-start.1 = (bf16[2048,512]{1,0:T(8,128)(2,1)S(1)}, bf16[2048,512]{1,0:T(8,128)(2,1)}, u32[]{:S(2)}) copy-start(bf16[2048,512]{1,0:T(8,128)(2,1)} %param.11) | copy-start | bytes 6291460
Sparse Core Ops, SparseCore 0:
  14.9 129.5 all-gather.9
  146.7 125.0 all-gather.7
  274.1 152.9 all-gather.5
  429.1 125.9 all-gather.11
  590.9 52.4 reduce-scatter.1

commit v2 on v1

--- a/solution.py
+++ b/solution.py
@@ -49,16 +49,184 @@
     return (attended * lax.rsqrt(mean_square + 1e-05) * gain).astype(jnp.bfloat16)
 
 
+def head_block(which, head):
+    return which, 0, head
+
+
 def head_kernel(local_bits, q_ref, k_ref, v_ref, weight_ref, partner_ref, gain_ref, out_ref):
     out_ref[...] = head_rows(
         local_bits,
-        q_ref[...],
-        k_ref[...],
-        v_ref[...],
+        q_ref[0],
+        k_ref[0],
+        v_ref[0],
         weight_ref[0],
         [partner_ref[n, 0] for n in range(partner_ref.shape[0])],
         gain_ref[...],
     )
+
+
+MESH = pl.DeviceIdType.MESH
+
+
+def spread_kernel(lanes, pieces, w_ref, out_ref, zr, yr, cr, down, up, ys, cs, own):
+    docs_at, seq_at = lax.axis_index("doc"), lax.axis_index("seq")
+    line = lax.axis_size("seq") // lanes
+    z, lane = seq_at // lanes, seq_at % lanes
+    units = w_ref.shape[0] * pieces
+    half_rows = w_ref.shape[1] // 2
+    rows = half_rows // pieces
+    count = (line - 1) * units
+
+    def row_slice(unit, half):
+        start = half * half_rows + unit % pieces * rows
+        return pl.ds(pl.multiple_of(start, 16), rows)
+
+    def slot(source, unit, half):
+        return out_ref.at[unit // pieces, source * lanes + lane, row_slice(unit, half)]
+
+    def shard(unit, half):
+        return w_ref.at[unit // pieces, row_slice(unit, half)]
+
+    def z_copy(source, unit, is_own, step, send):
+        src = shard(unit, docs_at) if is_own else slot(source, unit, docs_at)
+        return pltpu.make_async_remote_copy(
+            src, slot(source, unit, docs_at), send.at[source, unit], zr.at[source, unit],
+            device_id={"seq": seq_at + step * lanes}, device_id_type=MESH,
+        )
+
+    def y_copy(source, unit, half):
+        return pltpu.make_async_remote_copy(
+            slot(source, unit, half), slot(source, unit, half), ys.at[source, unit],
+            yr.at[source, unit], device_id={"doc": 1 - docs_at}, device_id_type=MESH,
+        )
+
+    def core_copy(source, unit, half, is_own):
+        src = shard(unit, half) if is_own else slot(source, unit, half)
+        return pltpu.make_async_remote_copy(
+            src, slot(source, unit, half), cs.at[source, unit, half], cr.at[source, unit, half],
+            device_id={"seq": z * lanes + (lanes - 1 - lane)}, device_id_type=MESH,
+        )
+
+    def core_arrival(source, unit, half):
+        there = out_ref.at[unit // pieces, source * lanes + (lanes - 1 - lane), row_slice(unit, half)]
+        return pltpu.make_async_remote_copy(
+            there, there, cs.at[source, unit, half], cr.at[source, unit, half],
+            device_id={"seq": z * lanes + (lanes - 1 - lane)}, device_id_type=MESH,
+        )
+
+    barrier = pltpu.get_barrier_semaphore()
+
+    def greet(**where):
+        pl.semaphore_signal(barrier, inc=1, device_id=where, device_id_type=MESH)
+
+    pl.when(z > 0)(lambda: greet(seq=seq_at - lanes))
+    pl.when(z < line - 1)(lambda: greet(seq=seq_at + lanes))
+    greet(doc=1 - docs_at)
+    if lanes == 2:
+        greet(seq=z * lanes + (lanes - 1 - lane))
+    edges = (z > 0).astype(jnp.int32) + (z < line - 1).astype(jnp.int32)
+    pl.semaphore_wait(barrier, edges + lanes)
+
+    own_copies = [
+        pltpu.make_async_copy(w_ref.at[k], out_ref.at[k, seq_at], own.at[k])
+        for k in range(w_ref.shape[0])
+    ]
+
+    def sends(position, begin):
+        unit, hop = position % units, position // units
+        for step, send in ((-1, down), (1, up)):
+            source = z - step * hop
+            target = z + step
+            there = (target >= 0) & (target < line)
+            there = there & (source >= 0) & (source < line)
+            there = there & (position >= 0) & (position < count)
+            for is_own in (True, False):
+                first = (hop == 0) if is_own else (hop > 0)
+
+                @pl.when(there & first)
+                def _():
+                    copy = z_copy(source, unit, is_own, step, send)
+                    copy.start() if begin else copy.wait_send()
+
+    def arrivals(position, act):
+        unit, hop = position % units, position // units
+        for step in (-1, 1):
+            source = z - step * (hop + 1)
+            there = (source >= 0) & (source < line) & (position >= 0) & (position < count)
+
+            @pl.when(there)
+            def _():
+                act(source, unit, step)
+
+    def on_z(source, unit, step):
+        z_copy(source, unit, False, -step, down).wait_recv()
+        y_copy(source, unit, docs_at).start()
+        if lanes == 2:
+            core_copy(source, unit, docs_at, False).start()
+
+    def on_y(source, unit, step):
+        y_copy(source, unit, 1 - docs_at).wait_recv()
+        if lanes == 2:
+            core_copy(source, unit, 1 - docs_at, False).start()
+
+    lag = jnp.where((z == 0) | (z == line - 1), 1, units)
+
+    def turn(t, carry):
+        sends(t - 2, False)
+        sends(t, True)
+        arrivals(t - 2, on_z)
+        arrivals(t - 2 - lag, on_y)
+
+        @pl.when(t == 1)
+        def _():
+            for copy in own_copies:
+                copy.start()
+
+        if lanes == 2:
+
+            @pl.when(t < units)
+            def _():
+                core_copy(z, t, 0, True).start()
+                core_copy(z, t, 1, True).start()
+
+        return carry
+
+    lax.fori_loop(0, count + 2 + units, turn, 0)
+
+    def finish(n, carry):
+        source, unit = n // units, n % units
+        pl.when(source != z)(lambda: y_copy(source, unit, docs_at).wait_send())
+        if lanes == 2:
+            for half in (0, 1):
+                core_arrival(source, unit, half).wait_recv()
+                core_copy(source, unit, half, False).wait_send()
+        return carry
+
+    lax.fori_loop(0, line * units, finish, 0)
+    for copy in own_copies:
+        copy.wait()
+
+
+def spread(w_qkv):
+    seqs = lax.axis_size("seq")
+    lanes = 2 if lax.axis_size("sub") == 1 and seqs % 2 == 0 else 1
+    line = seqs // lanes
+    pieces = 2 if line <= 4 else 1
+    units = w_qkv.shape[0] * pieces
+    sem = pltpu.SemaphoreType.DMA
+    core = (line, units, 2) if lanes == 2 else (1, 1, 1)
+    return pl.pallas_call(
+        functools.partial(spread_kernel, lanes, pieces),
+        out_shape=jax.ShapeDtypeStruct(
+            (w_qkv.shape[0], seqs) + w_qkv.shape[1:], jnp.bfloat16
+        ),
+        in_specs=[pl.BlockSpec(memory_space=pl.ANY)],
+        out_specs=pl.BlockSpec(memory_space=pl.ANY),
+        scratch_shapes=[sem((line, units)), sem((line, units)), sem(core)]
+        + [sem((line, units))] * 3
+        + [sem(core), sem((w_qkv.shape[0],))],
+        compiler_params=pltpu.CompilerParams(collective_id=0, has_side_effects=True),
+    )(w_qkv)
 
 
 def gathered(weight, axis):
@@ -77,30 +245,31 @@
     ).astype(jnp.bfloat16)
     head_cols = w_qkv.shape[2]
     groups_here = tok_rows // GROUP
-    swapped = normed.reshape(tok_rows, seqs, docs, -1).swapaxes(1, 2).reshape(tok_rows, width)
-
-    def project(which):
-        matrix = gathered(w_qkv[which], 0).reshape(width, head_cols)
-        return jnp.dot(swapped, matrix, preferred_element_type=jnp.float32).astype(jnp.bfloat16)
-
-    key_rows, values, queries = project(1), project(2), project(0)
-    w_out, _ = lax.optimization_barrier((w_out, values))
+    if docs == 2 and seqs > 1:
+        every = spread(w_qkv)
+    else:
+        every = lax.all_gather(w_qkv, "seq", axis=1)
+    w_out, every = lax.optimization_barrier((w_out, every))
     out_matrix = gathered(w_out, 0)
-    return attend(
-        widened, queries, key_rows, values, level_index, head_gain, out_matrix, groups_here
-    )
-
-
-def attend(widened, queries, key_rows, values, level_index, head_gain, out_matrix, groups_here):
-    tok_rows = queries.shape[0]
-    heads_here = queries.shape[1] // HD
+    projected = jnp.einsum(
+        "td,kdc->ktc",
+        normed,
+        every.reshape(-1, width, head_cols),
+        preferred_element_type=jnp.float32,
+    ).astype(jnp.bfloat16)
+    return attend(widened, projected, level_index, head_gain, out_matrix, groups_here)
+
+
+def attend(widened, projected, level_index, head_gain, out_matrix, groups_here):
+    tok_rows = projected.shape[1]
+    heads_here = projected.shape[2] // HD
     level_weight = jnp.zeros(level_index.shape, jnp.float32)
     for entry in range(len(TABLE)):
         level_weight = level_weight + jnp.where(level_index == entry, TABLE[entry], 0.0)
     totals = jnp.einsum(
         "thi,thj->hij",
-        key_rows.reshape(tok_rows, heads_here, HD),
-        values.reshape(tok_rows, heads_here, HD),
+        projected[1].reshape(tok_rows, heads_here, HD),
+        projected[2].reshape(tok_rows, heads_here, HD),
         preferred_element_type=jnp.float32,
     )
     local_bits = groups_here.bit_length() - 1
@@ -120,7 +289,9 @@
     head_normed = pl.pallas_call(
         functools.partial(head_kernel, local_bits),
         grid=(heads_here,),
-        in_specs=[pl.BlockSpec((tok_rows, HD), lambda h: (0, h))] * 3
+        in_specs=[
+            pl.BlockSpec((1, tok_rows, HD), functools.partial(head_block, k)) for k in range(3)
+        ]
         + [
             pl.BlockSpec((1,) + row_weights.shape[1:], lambda h: (h, 0, 0)),
             pl.BlockSpec((seq_bits, 1, HD, HD), lambda h: (0, h, 0, 0)),
@@ -134,7 +305,7 @@
             bytes_accessed=tok_rows * heads_here * HD * 12,
             transcendentals=0,
         ),
-    )(queries, key_rows, values, row_weights, jnp.stack(partners), head_gain[None, :])
+    )(projected, projected, projected, row_weights, jnp.stack(partners), head_gain[None, :])
     docs = lax.axis_size("doc")
     split_rows = head_normed.reshape(tok_rows, docs, heads_here * HD // docs)
     local_terms = jnp.einsum(

time: 656 us -> 498 us (0.76)
  waiting for transfers between devices: 485 us -> 145 us
  Pallas kernels: 13.1 us -> 237 us
  local copies, waits for them, and re-layouts: 60.2 us -> 34.2 us
  matrix products: 58.7 us -> 48.5 us
  other arithmetic: 23.2 us -> 15.5 us
    all_gather x4 -> x1, waiting for transfers between devices: 404 us -> 0.02 us  [gathered(): return lax.all_gather(mine, ('doc', 'seq'), axis=0)]
    pallas_call x0 -> x1, Pallas kernels: none -> 224 us  [spread(): pl.pallas_call(functools.partial(spread_kernel, lanes, pieces), out_shape...]
    ppermute x3, waiting for transfers between devices: 35.6 us -> 97.5 us  [partner_2(): return lax.ppermute(value, axis, pairs)]
    reshape x3 -> x0, local copies, waits for them, and re-layouts: 21.6 us -> none  [the longest x2 19 us: body(): normed.reshape(tok_rows, seqs, docs, -1).swapaxes(1, 2)]
    dot_general x4 -> x2, matrix products: 44.8 us -> 34.7 us  [the longest x1 31.9 us: body(): jnp.einsum('td,kdc->ktc', normed, every.reshape(-1, width, head_cols), pr...]
    dynamic_slice x4 -> x1, local copies, waits for them, and re-layouts: 8.03 us -> 1.04 us  [gathered(): lax.dynamic_slice_in_dim(weight, lax.axis_index('doc') * part, part, axis)]
  transfers between devices with their start and end apart: 8 -> 5, of which waited for: 7 -> 4; matrix products, arithmetic and copies ran while one was open for 14% -> 11% of each run, Pallas kernels for 2% -> 3%
where the time goes in v2:
time: 498 us; the launch traced here: 497 us
  Pallas kernels  237 us (48%)
  waiting for transfers between devices  145 us (29%)
  matrix products  48.5 us (10%)
  local copies, waits for them, and re-layouts  34.2 us (7%)
  other arithmetic  15.5 us (3%)
  between operations  13.6 us (3%)
    pallas_call x1, Pallas kernels, spread(): pl.pallas_call(functools.partial(spread_kernel, lanes, pieces), out_shape...  224 us
    ppermute x3, waiting for transfers between devices, partner_2(): return lax.ppermute(value, axis, pairs)  97.5 us
    reduce_scatter x1, waiting for transfers between devices, attend(): lax.psum_scatter(local_terms.astype(jnp.bfloat16), ('head', 'sub'), scatt...  47.8 us
    dot_general x1, matrix products, body(): jnp.einsum('td,kdc->ktc', normed, every.reshape(-1, width, head_cols), pr...  31.9 us
    reshape x1, local copies, waits for them, and re-layouts, attend(): out_matrix.reshape(docs, -1, *out_matrix.shape[1:])  21.7 us
    dot_general x1, matrix products, attend(): jnp.einsum('tyk,yskc->tsc', split_rows, out_matrix.reshape(docs, -1, *out...  13.8 us
    pallas_call x1, Pallas kernels, attend(): pl.pallas_call(functools.partial(head_kernel, local_bits), grid=(heads_he...  12.9 us
  transfers between devices with their start and end apart: 5, of which 4 were waited for; matrix products, arithmetic and copies ran while one was open for 11% of the time, Pallas kernels for 3%

profile of v2, /device:TPU:0, one launch (start us, length us, event | category | flops | bytes accessed | tf_op | source)
XLA Modules:
  0.0 496.8 jit_solution(10895379449251240683)
XLA Ops:
  6.5 0.0 copy-start
  6.5 0.0 all-gather.3.cloned.1.call-start
  6.5 224.3 %shard_map.64 = bf16[3,8,512,2048]{3,2,1,0:T(8,128)(2,1)} custom-call(bf16[3,512,2048]{2,1,0:T(8,128)(2,1)} %w_ref.1), custom_call_target="tpu_custom_call" | custom-call | tf_op jit(solution)/shard_map/pallas_call | solution.py:218
  230.8 0.0 copy-start.7
  230.8 0.0 copy-done
  230.9 1.0 constant_dynamic-slice_fusion
  231.9 0.0 all-gather.3.cloned.1.call-update
  231.9 0.0 reduce-scatter.2.cloned.1.call-start
  232.0 0.0 copy-start.5
  232.0 3.2 multiply_reduce_fusion
  235.2 0.0 copy-done.7
  235.2 0.2 copy-done.5
  235.4 31.9 %convert_bitcast_fusion.q_ref.k_ref.v_ref = bf16[3,512,2048]{2,1,0:T(8,128)(2,1)S(1)} fusion(bf16[3,4096,2048]{2,1,0:T(8,128)(2,1)} %bitcast.34, f32[4096]{0:T(1024)S(1)} %copy-done.7, f32[512]{0:T(512)S(1)} %add_rsqrt_fusion, bf16[512,4096]{1,0:T(8,128)(2,1)S(1)} %copy-done.5), kind=kOutput, calls=%fused_computation.3 | convolution fusion | flops 25781338112 | bytes 60835840 | tf_op jit(solution)/shard_map/td,kdc->ktc/dot_general | solution.py:254
  267.4 0.0 copy-start.2
  267.4 2.3 slice_bitcast_fusion
  269.7 1.0 copy-done.2
  270.7 0.6 copy.18
  271.3 4.0 copy.16
  275.3 0.0 copy-start.6
  275.3 2.8 fusion.10
  278.0 0.5 collective-permute-start
  278.5 1.5 collective-permute-done
  280.0 0.2 fusion.9
  280.2 1.6 collective-permute-start.1
  281.8 45.0 %collective-permute-done.1 = bf16[16,128,128]{2,1,0:T(8,128)(2,1)S(1)} collective-permute-done((bf16[16,128,128]{2,1,0:T(8,128)(2,1)S(1)}, bf16[16,128,128]{2,1,0:T(8,128)(2,1)S(1)}, u32[]{:S(2)}, u32[]{:S(2)}) %collective-permute-start.1) | collective-permute-done | bytes 524320 | tf_op jit(solution)/shard_map/ppermute | solution.py:20
  326.8 0.2 add_convert_fusion.1
  327.0 0.0 copy-start.4
  327.0 0.4 collective-permute-start.2
  327.4 0.1 convert_multiply_fusion
  327.5 0.0 copy-done.6
  327.5 0.1 multiply_bitcast_fusion
  327.5 0.1 copy.9
  327.7 51.0 %collective-permute-done.2 = bf16[16,128,128]{2,1,0:T(8,128)(2,1)S(1)} collective-permute-done((bf16[16,128,128]{2,1,0:T(8,128)(2,1)S(1)}, bf16[16,128,128]{2,1,0:T(8,128)(2,1)S(1)}, u32[]{:S(2)}, u32[]{:S(2)}) %collective-permute-start.2) | collective-permute-done | bytes 524320 | tf_op jit(solution)/shard_map/ppermute | solution.py:20
  378.7 0.2 pad_maximum_fusion.partner_ref
  378.8 0.3 broadcast_in_dim.54
  379.1 0.0 copy-done.4
  379.1 0.0 copy-start.3
  379.1 3.0 copy-done.3
  382.1 12.9 %shard_map.65 = bf16[512,2048]{1,0:T(8,128)(2,1)S(1)} custom-call(bf16[3,512,2048]{2,1,0:T(8,128)(2,1)S(1)} %copy-done.3, bf16[3,512,2048]{2,1,0:T(8,128)(2,1)S(1)} %copy-done.3, bf16[3,512,2048]{2,1,0:T(8,128)(2,1)S(1)} %copy-done.3, f32[16,512,7]{2,1,0:T(8,128)S(1)} %bitcast.31, bf16[3,16,128,128]{3,2,1,0:T(8,128)(2,1)S(1)} %pad_maximum_fusion.partner_ref, ...), custom_call_target="tpu_custom_call" | custom-call | flops 3758096384 | bytes 12582912 | tf_op jit(solution)/shard_map/pallas_call | solution.py:289
  395.0 0.0 all-gather.3.cloned.1.call-done
  395.0 21.7 %copy.12 = bf16[2,8,1024,512]{2,3,1,0:T(8,128)(2,1)} copy(bf16[2,8,1024,512]{3,2,1,0:T(8,128)(2,1)} %bitcast.35) | data formatting | bytes 33554432 | tf_op jit(solution)/shard_map/reshape | solution.py:314
  416.7 13.8 %bitcast_convert_fusion = bf16[512,4096]{1,0:T(8,128)(2,1)} fusion(bf16[4096,1024,2]{1,0,2:T(8,128)(2,1)} %bitcast.36, bf16[64,2,8,1024]{3,2,1,0:T(8,128)(2,1)S(1)} %bitcast.32), kind=kOutput, calls=%fused_computation | convolution fusion | flops 8592031744 | bytes 23068672 | tf_op jit(solution)/shard_map/tyk,yskc->tsc/dot_general | solution.py:311
  430.6 0.0 reduce-scatter.2.cloned.1.call-update
  430.6 6.7 %convert_element_type.38 = f32[512,4096]{1,0:T(8,128)} convert(bf16[512,4096]{1,0:T(8,128)(2,1)} %param.6) | non-fusion elementwise | flops 2097152 | bytes 12582912 | tf_op jit(solution)/shard_map/convert_element_type | solution.py:242
  437.3 0.0 copy-start.1
  437.3 47.8 %reduce-scatter.2.cloned.1.call-done = bf16[512,2048]{1,0:T(8,128)(2,1)} async-done(((bf16[512,4096]{1,0:T(8,128)(2,1)}), bf16[512,2048]{1,0:T(8,128)(2,1)}) %reduce-scatter.2.cloned.1.call-update) | async-done | bytes 2097168 | tf_op jit(solution)/shard_map/reduce_scatter | solution.py:318
  485.1 4.8 add_convert_fusion
  490.0 0.0 copy-done.1
  (2 shorter events, 0.0 us)
Async XLA Ops:
  6.5 224.3 %copy-start = (bf16[2048,512]{1,0:T(8,128)(2,1)S(1)}, bf16[2048,512]{1,0:T(8,128)(2,1)}, u32[]{:S(2)}) copy-start(bf16[2048,512]{1,0:T(8,128)(2,1)} %param.11) | copy-start | bytes 6291460
  6.5 388.5 %all-gather.3.cloned.1.call-start = ((), (), s32[]{:S(2)}) async-start(), calls=%async_computation.2 | async-start | bytes 17825792 | tf_op jit(solution)/shard_map/all_gather | solution.py:236
  230.8 4.4 copy-start.7
  231.9 253.2 %reduce-scatter.2.cloned.1.call-start = ((), (), s32[]{:S(2)}) async-start(), calls=%async_computation.1 | async-start | bytes 6291456 | tf_op jit(solution)/shard_map/reduce_scatter | solution.py:318
  232.0 3.5 copy-start.5
  267.4 3.3 copy-start.2
  275.3 52.2 %copy-start.6 = (s32[8,16,7]{1,0,2:T(8,128)S(1)}, s32[8,16,7]{1,0,2:T(8,128)}, u32[]{:S(2)}) copy-start(s32[8,16,7]{1,0,2:T(8,128)} %param.9) | copy-start | bytes 10756
  278.0 2.0 collective-permute-start
  280.2 46.6 %collective-permute-start.1 = (bf16[16,128,128]{2,1,0:T(8,128)(2,1)S(1)}, bf16[16,128,128]{2,1,0:T(8,128)(2,1)S(1)}, u32[]{:S(2)}, u32[]{:S(2)}) collective-permute-start(bf16[16,128,128]{2,1,0:T(8,128)(2,1)S(1)} %fusion.9), channel_id=1, source_target_pairs={{0,4},{2,6},{4,0},{6,2},{8,12},{10,14},{12,8},{14,10},{1,5},{3,7},... | collective-permute-start | bytes 1572872 | tf_op jit(solution)/shard_map/ppermute | solution.py:20
  327.0 52.1 %copy-start.4 = (f32[2048]{0:T(1024)S(1)}, f32[2048]{0:T(1024)}, u32[]{:S(2)}) copy-start(f32[2048]{0:T(1024)} %param.10) | copy-start | bytes 24580
  327.0 51.7 %collective-permute-start.2 = (bf16[16,128,128]{2,1,0:T(8,128)(2,1)S(1)}, bf16[16,128,128]{2,1,0:T(8,128)(2,1)S(1)}, u32[]{:S(2)}, u32[]{:S(2)}) collective-permute-start(bf16[16,128,128]{2,1,0:T(8,128)(2,1)S(1)} %add_convert_fusion.1), channel_id=1, source_target_pairs={{0,8},{2,10},{4,12},{6,14},{8,0},{10,2},{12,4},{14,6},{1,9},{3,11}... | collective-permute-start | bytes 1572872 | tf_op jit(solution)/shard_map/ppermute | solution.py:20
  379.1 3.0 copy-start.3
  437.3 52.7 %copy-start.1 = (bf16[2048,512]{1,0:T(8,128)(2,1)S(1)}, bf16[2048,512]{1,0:T(8,128)(2,1)}, u32[]{:S(2)}) copy-start(bf16[2048,512]{1,0:T(8,128)(2,1)} %param.11) | copy-start | bytes 6291460
Sparse Core Ops, SparseCore 0:
  232.0 148.9 all-gather.2
  430.7 54.3 reduce-scatter.1

commit v3 on v2

--- a/solution.py
+++ b/solution.py
@@ -229,11 +229,11 @@
     )(w_qkv)
 
 
-def gathered(weight, axis):
+def gathered_columns(w_out):
     docs = lax.axis_size("doc")
-    part = weight.shape[axis] // docs
-    mine = lax.dynamic_slice_in_dim(weight, lax.axis_index("doc") * part, part, axis)
-    return lax.all_gather(mine, ("doc", "seq"), axis=0)
+    part = w_out.shape[1] // docs
+    mine = lax.dynamic_slice_in_dim(w_out, lax.axis_index("doc") * part, part, 1)
+    return lax.all_gather(mine.T, ("seq", "doc"), axis=0, tiled=True)
 
 
 def body(tokens, pre_gain, w_qkv, level_index, head_gain, w_out):
@@ -250,7 +250,7 @@
     else:
         every = lax.all_gather(w_qkv, "seq", axis=1)
     w_out, every = lax.optimization_barrier((w_out, every))
-    out_matrix = gathered(w_out, 0)
+    out_matrix = gathered_columns(w_out)
     projected = jnp.einsum(
         "td,kdc->ktc",
         normed,
@@ -276,11 +276,23 @@
     seq_bits = lax.axis_size("seq").bit_length() - 1
     position = lax.axis_index("seq")
     partners = []
-    block_sum = totals
+    block_sum, rounded = totals, totals.astype(jnp.bfloat16)
     for bit_index in range(seq_bits):
-        partner = partner_2(block_sum.astype(jnp.bfloat16), "seq", bit_index)
-        partners.append(partner)
-        block_sum = block_sum + partner.astype(jnp.float32)
+        if bit_index == seq_bits - 1 and bit_index > 0:
+            near = partner_2(previous, "seq", bit_index)
+            far = lax.ppermute(
+                previous,
+                "seq",
+                [(n, n ^ (3 << bit_index - 1)) for n in range(lax.axis_size("seq"))],
+            )
+            summed = near.astype(jnp.float32) + far.astype(jnp.float32)
+            partners.append(summed.astype(jnp.bfloat16))
+        else:
+            partner = partner_2(rounded, "seq", bit_index)
+            partners.append(partner)
+            previous = rounded
+            block_sum = block_sum + partner.astype(jnp.float32)
+            rounded = block_sum.astype(jnp.bfloat16)
     bits = jnp.arange(seq_bits, dtype=jnp.int32)
     used = jnp.concatenate(
         [jnp.ones((local_bits + 1,), jnp.int32), position >> bits & 1]
@@ -306,21 +318,29 @@
             transcendentals=0,
         ),
     )(projected, projected, projected, row_weights, jnp.stack(partners), head_gain[None, :])
-    docs = lax.axis_size("doc")
-    split_rows = head_normed.reshape(tok_rows, docs, heads_here * HD // docs)
-    local_terms = jnp.einsum(
-        "tyk,yskc->tsc",
-        split_rows,
-        out_matrix.reshape(docs, -1, *out_matrix.shape[1:]),
-        preferred_element_type=jnp.float32,
-    ).reshape(tok_rows, -1)
-    feature_cols = local_terms.shape[1] // lax.axis_size(("head", "sub"))
-    summed = lax.psum_scatter(
-        local_terms.astype(jnp.bfloat16), ("head", "sub"), scatter_dimension=1, tiled=True
-    ).astype(jnp.float32)
-    residual = lax.dynamic_slice_in_dim(
-        widened, lax.axis_index(("head", "sub")) * feature_cols, feature_cols, 1
-    )
+    axes = ("head", "sub")
+    shares = lax.axis_size(axes)
+    feature_cols = out_matrix.shape[0] // shares
+    mine = lax.axis_index(axes)
+
+    def terms(share):
+        part = lax.dynamic_slice_in_dim(out_matrix, share * feature_cols, feature_cols, 0)
+        return lax.dot_general(
+            head_normed, part, (((1,), (1,)), ((), ())), preferred_element_type=jnp.float32
+        )
+
+    residual = lax.dynamic_slice_in_dim(widened, mine * feature_cols, feature_cols, 1)
+    if shares == 2:
+        theirs = terms(1 - mine).astype(jnp.bfloat16)
+        arrived = lax.ppermute(theirs, axes, [(0, 1), (1, 0)])
+        summed = terms(mine) + arrived.astype(jnp.float32)
+    else:
+        local_terms = lax.dot_general(
+            head_normed, out_matrix, (((1,), (1,)), ((), ())), preferred_element_type=jnp.float32
+        )
+        summed = lax.psum_scatter(
+            local_terms.astype(jnp.bfloat16), axes, scatter_dimension=1, tiled=True
+        ).astype(jnp.float32)
     return (residual + summed).astype(jnp.bfloat16)
 
 

time: 498 us -> 479 us (0.962)
  local copies, waits for them, and re-layouts: 34.2 us -> 10.2 us
  matrix products: 48.5 us -> 55.7 us
    reduce_scatter x1 -> x0, waiting for transfers between devices: 47.8 us -> none  [attend(): lax.psum_scatter(local_terms.astype(jnp.bfloat16), ('head', 'sub'), scatt...]
    ppermute x0 -> x2, waiting for transfers between devices: none -> 39.9 us  [the longest x1 39.9 us: attend(): arrived = lax.ppermute(theirs, axes, [(0, 1), (1, 0)])]
    all_gather x1, waiting for transfers between devices: 0.02 us -> 35.4 us  [gathered_columns(): return lax.all_gather(mine.T, ('seq', 'doc'), axis=0, tiled=True)]
    ppermute x3, waiting for transfers between devices: 97.5 us -> 66.7 us  [partner_2(): return lax.ppermute(value, axis, pairs)]
    reshape x1 -> x0, local copies, waits for them, and re-layouts: 21.7 us -> none  [attend(): out_matrix.reshape(docs, -1, *out_matrix.shape[1:])]
    dot_general x1 -> x2, matrix products: 13.8 us -> 20.3 us  [terms(): lax.dot_general(head_normed, part, (((1,), (1,)), ((), ())), preferred_el...]
  transfers between devices with their start and end apart: 5 -> 6, of which waited for: 4 -> 4; matrix products, arithmetic and copies ran while one was open for 11% -> 11% of each run, Pallas kernels for 3% -> 3%
where the time goes in v3:
time: 479 us; the launch traced here: 478 us
  Pallas kernels  237 us (49%)
  waiting for transfers between devices  142 us (30%)
  matrix products  55.7 us (12%)
  between operations  13.6 us (3%)
  other arithmetic  13.3 us (3%)
  local copies, waits for them, and re-layouts  10.2 us (2%)
  starting transfers between devices  5.9 us (1%)
    pallas_call x1, Pallas kernels, spread(): pl.pallas_call(functools.partial(spread_kernel, lanes, pieces), out_shape...  224 us
    ppermute x3, waiting for transfers between devices, partner_2(): return lax.ppermute(value, axis, pairs)  66.7 us
    ppermute x1, waiting for transfers between devices, attend(): arrived = lax.ppermute(theirs, axes, [(0, 1), (1, 0)])  39.9 us
    all_gather x1, waiting for transfers between devices, gathered_columns(): return lax.all_gather(mine.T, ('seq', 'doc'), axis=0, tiled=True)  35.4 us
    dot_general x1, matrix products, body(): jnp.einsum('td,kdc->ktc', normed, every.reshape(-1, width, head_cols), pr...  31.9 us
    dot_general x2, matrix products, terms(): lax.dot_general(head_normed, part, (((1,), (1,)), ((), ())), preferred_el...  20.3 us
    pallas_call x1, Pallas kernels, attend(): pl.pallas_call(functools.partial(head_kernel, local_bits), grid=(heads_he...  13.1 us
  transfers between devices with their start and end apart: 6, of which 4 were waited for; matrix products, arithmetic and copies ran while one was open for 11% of the time, Pallas kernels for 3%

profile of v3, /device:TPU:0, one launch (start us, length us, event | category | flops | bytes accessed | tf_op | source)
XLA Modules:
  0.0 478.0 jit_solution(6544444065997376495)
XLA Ops:
  6.5 0.0 copy-start
  6.5 0.0 all-gather.2.cloned.1.call-start
  6.5 224.3 %shard_map.64 = bf16[3,8,512,2048]{3,2,1,0:T(8,128)(2,1)} custom-call(bf16[3,512,2048]{2,1,0:T(8,128)(2,1)} %w_ref.1), custom_call_target="tpu_custom_call" | custom-call | tf_op jit(solution)/shard_map/pallas_call | solution.py:218
  230.8 0.0 copy-start.7
  230.8 0.0 copy-done
  230.9 1.0 dynamic-slice_bitcast_fusion
  231.9 0.0 all-gather.2.cloned.1.call-update
  231.9 0.0 copy-start.5
  231.9 3.2 multiply_reduce_fusion
  235.2 0.0 copy-done.7
  235.2 0.2 copy-done.5
  235.4 31.9 %convert_bitcast_fusion.q_ref.k_ref.v_ref = bf16[3,512,2048]{2,1,0:T(8,128)(2,1)S(1)} fusion(bf16[3,4096,2048]{2,1,0:T(8,128)(2,1)} %bitcast.29, f32[4096]{0:T(1024)S(1)} %copy-done.7, f32[512]{0:T(512)S(1)} %add_rsqrt_fusion, bf16[512,4096]{1,0:T(8,128)(2,1)S(1)} %copy-done.5), kind=kOutput, calls=%fused_computation.6 | convolution fusion | flops 25781338112 | bytes 60835840 | tf_op jit(solution)/shard_map/td,kdc->ktc/dot_general | solution.py:254
  267.3 0.0 copy-start.2
  267.3 0.5 slice_bitcast_fusion
  267.8 2.2 copy-done.2
  270.0 2.0 copy.15
  272.0 2.5 copy.14
  274.5 0.0 copy-start.6
  274.5 0.0 slice-start
  274.5 3.5 fusion.19
  278.0 0.5 collective-permute-start
  278.5 1.5 collective-permute-done
  280.0 0.9 add_convert_fusion.2
  280.9 3.0 collective-permute-start.2
  283.9 0.9 collective-permute-start.3
  284.8 0.0 collective-permute-start.1
  284.8 0.1 convert_multiply_fusion
  284.9 0.0 copy-done.6
  284.9 0.1 multiply_bitcast_fusion
  285.0 0.1 copy.9
  285.1 0.0 slice-start.1
  285.1 0.0 copy-start.4
  285.1 65.1 %collective-permute-done.2 = bf16[16,128,128]{2,1,0:T(8,128)(2,1)S(1)} collective-permute-done((bf16[16,128,128]{2,1,0:T(8,128)(2,1)}, bf16[16,128,128]{2,1,0:T(8,128)(2,1)S(1)}, u32[]{:S(2)}, u32[]{:S(2)}) %collective-permute-start.2) | collective-permute-done | bytes 524320 | tf_op jit(solution)/shard_map/ppermute | solution.py:20
  350.3 0.0 collective-permute-done.3
  350.3 1.2 fusion.14
  351.5 0.0 collective-permute-done.1
  351.5 1.2 pad_maximum_fusion.partner_ref
  352.7 0.3 broadcast_in_dim.54
  353.0 0.0 slice-done
  353.0 0.0 slice-done.1
  353.0 0.0 copy-done.4
  353.0 13.1 %shard_map.65 = bf16[512,2048]{1,0:T(8,128)(2,1)S(1)} custom-call(bf16[3,512,2048]{2,1,0:T(8,128)(2,1)S(1)} %bitcast.26, bf16[3,512,2048]{2,1,0:T(8,128)(2,1)S(1)} %bitcast.26, bf16[3,512,2048]{2,1,0:T(8,128)(2,1)S(1)} %bitcast.26, f32[16,512,7]{2,1,0:T(8,128)S(1)} %bitcast.27, bf16[3,16,128,128]{3,2,1,0:T(8,128)(2,1)S(1)} %pad_maximum_fusion.partner_ref, ...), custom_call_target="tpu_custom_call" | custom-call | flops 3758096384 | bytes 12582912 | tf_op jit(solution)/shard_map/pallas_call | solution.py:301
  366.1 0.0 copy-start.3
  366.1 1.4 copy-done.3
  367.5 35.4 %all-gather.2.cloned.1.call-done = bf16[4096,2048]{0,1:T(8,128)(2,1)} async-done(((bf16[256,2048]{0,1:T(8,128)(2,1)}), bf16[4096,2048]{0,1:T(8,128)(2,1)}) %all-gather.2.cloned.1.call-update) | async-done | bytes 16777232 | tf_op jit(solution)/shard_map/all_gather | solution.py:236
  402.9 8.5 %fusion.9 = bf16[512,2048]{1,0:T(8,128)(2,1)S(1)} fusion(bf16[512,2048]{1,0:T(8,128)(2,1)} %copy-done.3, bf16[4096,2048]{0,1:T(8,128)(2,1)} %all-gather.2.cloned.1.call-done, s32[]{:T(128)S(6)} %select_n.45), kind=kOutput, calls=%fused_computation.12 | convolution fusion | flops 4296015872 | bytes 12582916 | tf_op jit(solution)/shard_map/dot_general | solution.py:328
  411.4 1.6 collective-permute-start.4
  413.0 6.5 %convert_element_type.41 = f32[512,4096]{1,0:T(8,128)} convert(bf16[512,4096]{1,0:T(8,128)(2,1)} %param.6) | non-fusion elementwise | flops 2097152 | bytes 12582912 | tf_op jit(solution)/shard_map/convert_element_type | solution.py:242
  419.5 39.9 %collective-permute-done.4 = bf16[512,2048]{1,0:T(8,128)(2,1)} collective-permute-done((bf16[512,2048]{1,0:T(8,128)(2,1)S(1)}, bf16[512,2048]{1,0:T(8,128)(2,1)}, u32[]{:S(2)}, u32[]{:S(2)}) %collective-permute-start.4) | collective-permute-done | bytes 2097184 | tf_op jit(solution)/shard_map/ppermute | solution.py:335
  459.4 0.0 copy-start.1
  459.4 11.7 %add_convert_fusion = bf16[512,2048]{1,0:T(8,128)(2,1)} fusion(bf16[512,2048]{1,0:T(8,128)(2,1)} %collective-permute-done.4, f32[512,4096]{1,0:T(8,128)} %convert_element_type.41, s32[]{:T(128)S(6)} %select_n.35, bf16[512,2048]{1,0:T(8,128)(2,1)} %copy-done.3, bf16[4096,2048]{0,1:T(8,128)(2,1)} %all-gather.2.cloned.1.call-done), kind=kOutput, calls=%fused_computation.8 | convolution fusion | flops 4299161600 | bytes 18875392 | tf_op jit(solution)/shard_map/dot_general | solution.py:328
  471.1 0.0 copy-done.1
  (3 shorter events, 0.0 us)
Async XLA Ops:
  6.5 224.3 %copy-start = (bf16[2048,512]{1,0:T(8,128)(2,1)S(1)}, bf16[2048,512]{1,0:T(8,128)(2,1)}, u32[]{:S(2)}) copy-start(bf16[2048,512]{1,0:T(8,128)(2,1)} %param.11) | copy-start | bytes 6291460
  6.5 396.4 %all-gather.2.cloned.1.call-start = ((), (), s32[]{:S(2)}) async-start(), calls=%async_computation | async-start | bytes 17825792 | tf_op jit(solution)/shard_map/all_gather | solution.py:236
  230.8 4.4 copy-start.7
  231.9 3.5 copy-start.5
  267.3 2.7 copy-start.2
  274.5 10.4 %copy-start.6 = (s32[8,16,7]{1,0,2:T(8,128)S(1)}, s32[8,16,7]{1,0,2:T(8,128)}, u32[]{:S(2)}) copy-start(s32[8,16,7]{1,0,2:T(8,128)} %param.9) | copy-start | bytes 10756
  274.5 78.5 %slice-start = ((s8[6291456]{0:T(1024)(128)(4,1)}), s8[2097152]{0:T(1024)(128)(4,1)S(1)}, s32[]{:S(2)}) async-start(s8[6291456]{0:T(1024)(128)(4,1)} %bitcast.25), calls=%async_computation.1 | async-start | bytes 4194304
  278.0 2.0 collective-permute-start
  280.9 69.3 %collective-permute-start.2 = (bf16[16,128,128]{2,1,0:T(8,128)(2,1)}, bf16[16,128,128]{2,1,0:T(8,128)(2,1)S(1)}, u32[]{:S(2)}, u32[]{:S(2)}) collective-permute-start(bf16[16,128,128]{2,1,0:T(8,128)(2,1)} %add_convert_fusion.2), channel_id=1, source_target_pairs={{0,8},{2,10},{4,12},{6,14},{8,0},{10,2},{12,4},{14,6},{1,9},{3,11}... | collective-permute-start | bytes 1572872 | tf_op jit(solution)/shard_map/ppermute | solution.py:20
  283.9 66.3 %collective-permute-start.3 = (bf16[16,128,128]{2,1,0:T(8,128)(2,1)}, bf16[16,128,128]{2,1,0:T(8,128)(2,1)}, u32[]{:S(2)}, u32[]{:S(2)}) collective-permute-start(bf16[16,128,128]{2,1,0:T(8,128)(2,1)} %add_convert_fusion.2), channel_id=1, source_target_pairs={{0,12},{2,14},{4,8},{6,10},{8,4},{10,6},{12,0},{14,2},{1,13},{3,15... | collective-permute-start | bytes 1572872 | tf_op jit(solution)/shard_map/ppermute | solution.py:283
  284.8 66.6 %collective-permute-start.1 = (bf16[16,128,128]{2,1,0:T(8,128)(2,1)}, bf16[16,128,128]{2,1,0:T(8,128)(2,1)}, u32[]{:S(2)}, u32[]{:S(2)}) collective-permute-start(bf16[16,128,128]{2,1,0:T(8,128)(2,1)} %add_convert_fusion.2), channel_id=1, source_target_pairs={{0,4},{2,6},{4,0},{6,2},{8,12},{10,14},{12,8},{14,10},{1,5},{3,7},... | collective-permute-start | bytes 1572872 | tf_op jit(solution)/shard_map/ppermute | solution.py:20
  285.1 67.9 %slice-start.1 = ((s8[6291456]{0:T(1024)(128)(4,1)}), s8[4194304]{0:T(1024)(128)(4,1)S(1)}, s32[]{:S(2)}) async-start(s8[6291456]{0:T(1024)(128)(4,1)} %bitcast.25), calls=%async_computation.2 | async-start | bytes 8388608
  285.1 67.9 %copy-start.4 = (f32[2048]{0:T(1024)S(1)}, f32[2048]{0:T(1024)}, u32[]{:S(2)}) copy-start(f32[2048]{0:T(1024)} %param.10) | copy-start | bytes 24580
  366.1 1.4 copy-start.3
  411.4 48.0 %collective-permute-start.4 = (bf16[512,2048]{1,0:T(8,128)(2,1)S(1)}, bf16[512,2048]{1,0:T(8,128)(2,1)}, u32[]{:S(2)}, u32[]{:S(2)}) collective-permute-start(bf16[512,2048]{1,0:T(8,128)(2,1)S(1)} %fusion.9), channel_id=1, source_target_pairs={{0,1},{1,0},{2,3},{3,2},{4,5},{5,4},{6,7},{7,6},{8,9},{9,8},{10,11... | collective-permute-start | bytes 6291464 | tf_op jit(solution)/shard_map/ppermute | solution.py:335
  459.4 11.8 %copy-start.1 = (bf16[2048,512]{1,0:T(8,128)(2,1)S(1)}, bf16[2048,512]{1,0:T(8,128)(2,1)}, u32[]{:S(2)}) copy-start(bf16[2048,512]{1,0:T(8,128)(2,1)} %param.11) | copy-start | bytes 6291460
Sparse Core Ops, SparseCore 0:
  232.0 170.8 all-gather.1
